TPU v7x, 128 devices: a whole 4x4x4 slice. The times are simulated.
128 devices in a mesh: row: 8 (over x, core), col: 16 (over z, y).
Axes of the slice: x: 4, y: 4, z: 4, core: 2. Of those that a mesh axis runs over, the one named last changes fastest.
Arguments:
- loaded: bfloat16 [1536, 8192], P('col', 'row'), may hold values from -6 to 6
- positions: int32 [1536], P('col'), may hold values from 0 to 1535, as said below
- gate_weight: bfloat16 [8192, 14336], P('row', 'col'), may hold values from -0.0625 to 0.0625
- up_weight: bfloat16 [8192, 14336], P('row', 'col'), may hold values from -0.0625 to 0.0625
- down_weight: bfloat16 [14336, 8192], P('col', 'row'), may hold values from -0.046875 to 0.046875
- segment: int32 [1536], P('col'), may hold values from 0 to 7, never falling along the last dimension, each value on 1 to 384 neighbouring positions
- log_ratio: float32 [1536], P('col'), may hold values from -6 to 6
- token_grad: bfloat16 [1536, 8192], P('col', 'row'), may hold values from -48 to 48
Outputs:
- mixed: bfloat16 [1536, 8192], P('col', 'row')
- grad_inputs: bfloat16 [1536, 8192], P('col', 'row')
- grad_gate: float32 [8192, 14336], P('row', 'col')
- grad_up: float32 [8192, 14336], P('row', 'col')
- grad_down: float32 [14336, 8192], P('col', 'row')
Inputs may be any that keep to these rules, and one draw needn't show every extreme that they name: positions is a permutation of the 1536 packed positions. Loader block c holds loader rows c * 96 to (c + 1) * 96 - 1 and owner block b holds positions b * 96 to (b + 1) * 96 - 1; at most 18 rows of one loader block land in one owner block, and every draw reaches 18.
All inputs are finite; a program needn't handle non-finite values.
Results may differ from a plain program's by a relative error of at most 0.033.
Values may be sent and summed in bfloat16 or wider, within the bound.
A program may use at most 128 MiB of HBM per device.

v0:
```python
import jax
import jax.numpy as jnp
from jax import lax
from jax.sharding import PartitionSpec as P

PAIRS = 4


BETA = 0.1


def per_device(
    loaded, positions, gate_weight, up_weight, down_weight, segment, log_ratio, token_grad
):
    rows_here = loaded.shape[0]
    peers = lax.axis_size("col")
    capacity = 3 * rows_here // peers
    owner_block = positions // rows_here
    local_place = positions % rows_here
    owner_table = (owner_block[:, None] == jnp.arange(peers, dtype=jnp.int32)[None, :]).astype(
        jnp.int32
    )
    earlier = jnp.cumsum(owner_table, 0) - owner_table
    order_rank = jnp.sum(earlier * owner_table, 1)
    flat_slot = owner_block * capacity + order_rank
    send_rows = (
        jnp.zeros((peers * capacity, loaded.shape[1]), loaded.dtype).at[flat_slot].set(loaded)
    )
    send_place = jnp.full((peers * capacity,), rows_here, jnp.int32).at[flat_slot].set(local_place)
    got_rows, got_place = (
        lax.all_to_all(send_rows, "col", split_axis=0, concat_axis=0, tiled=True),
        lax.all_to_all(send_place, "col", split_axis=0, concat_axis=0, tiled=True),
    )
    local_rows = jnp.zeros(loaded.shape, loaded.dtype).at[got_place].set(got_rows, mode="drop")
    inputs_all = lax.all_gather(local_rows, "col", axis=0, tiled=True)
    hidden_width = gate_weight.shape[1]
    both_weights = jnp.concatenate([gate_weight, up_weight], 1)
    contract_last = (((1,), (1,)), ((), ()))
    contract_first = (((0,), (0,)), ((), ()))
    row_block = inputs_all
    pre_acts = lax.psum_scatter(
        jnp.dot(row_block, both_weights, preferred_element_type=jnp.float32).astype(jnp.bfloat16),
        "row",
        scatter_dimension=0,
        tiled=True,
    ).astype(jnp.float32)
    gate_pre = pre_acts[:, :hidden_width]
    up_pre = pre_acts[:, hidden_width:]
    hidden_share = (jax.nn.silu(gate_pre) * up_pre).astype(jnp.bfloat16)
    hidden_all = lax.all_gather(hidden_share, "row", axis=0, tiled=True)
    row_block = hidden_all
    mixed = lax.psum_scatter(
        jnp.dot(row_block, down_weight, preferred_element_type=jnp.float32).astype(jnp.bfloat16),
        "col",
        scatter_dimension=0,
        tiled=True,
    )
    member = (segment[:, None] == jnp.arange(2 * PAIRS, dtype=jnp.int32)[None, :]).astype(
        jnp.float32
    )
    totals = lax.psum(jnp.sum(log_ratio[:, None] * member, 0), "col")
    margin = BETA * (totals[0::2] - totals[1::2])
    pair_weight = -BETA * jax.nn.sigmoid(-margin)
    signed = jnp.stack([pair_weight, -pair_weight], 1).reshape(-1)
    token_weight = jnp.sum(member * signed[None, :], 1)
    out_grad = (token_weight[:, None] * token_grad.astype(jnp.float32)).astype(jnp.bfloat16)
    grads_all = lax.all_gather(out_grad, "col", axis=0, tiled=True)
    row_block = grads_all
    grad_hidden = lax.psum_scatter(
        lax.dot_general(
            row_block, down_weight, contract_last, preferred_element_type=jnp.float32
        ).astype(jnp.bfloat16),
        "row",
        scatter_dimension=0,
        tiled=True,
    ).astype(jnp.float32)
    sigmoid_gate = jax.nn.sigmoid(gate_pre)
    act_gate = grad_hidden * up_pre * sigmoid_gate * (1.0 + gate_pre * (1.0 - sigmoid_gate))
    act_up = grad_hidden * gate_pre * sigmoid_gate
    act_share = jnp.concatenate([act_gate.astype(jnp.bfloat16), act_up.astype(jnp.bfloat16)], 1)
    act_all = lax.all_gather(act_share, "row", axis=0, tiled=True)
    grad_down = lax.dot_general(
        hidden_all, grads_all, contract_first, preferred_element_type=jnp.float32
    )
    grad_both = lax.dot_general(
        inputs_all, act_all, contract_first, preferred_element_type=jnp.float32
    )
    grad_gate = grad_both[:, :hidden_width]
    grad_up = grad_both[:, hidden_width:]
    row_block = act_all
    grad_inputs = lax.psum_scatter(
        lax.dot_general(
            row_block, both_weights, contract_last, preferred_element_type=jnp.float32
        ).astype(jnp.bfloat16),
        "col",
        scatter_dimension=0,
        tiled=True,
    )
    return (mixed, grad_inputs, grad_gate, grad_up, grad_down)


def solution(mesh):
    return jax.shard_map(
        per_device,
        mesh=mesh,
        in_specs=(
            P("col", "row"),
            P("col"),
            P("row", "col"),
            P("row", "col"),
            P("col", "row"),
            P("col"),
            P("col"),
            P("col", "row"),
        ),
        out_specs=(
            P("col", "row"),
            P("col", "row"),
            P("row", "col"),
            P("row", "col"),
            P("col", "row"),
        ),
        check_vma=False,
    )
```

profile of v0, /device:TPU:0, one launch (start us, length us, event | category | flops | bytes accessed | tf_op | source)
XLA Modules:
  0.0 454.4 jit_solution(9229231282478643345)
XLA Ops:
  7.2 0.0 copy-start
  7.2 0.8 and_select_fusion
  8.0 0.1 fusion.9
  8.1 0.1 reduce_window_sum.11
  8.2 0.2 select_reduce_fusion
  8.4 0.9 scatter_custom_fusion
  9.3 0.7 all_to_all.16
  10.0 8.1 %all-to-all-start = ((s32[16,18,1]{1,2,0:T(1,128)}), s32[16,18,1]{1,2,0:T(1,128)S(1)}, u32[]{:S(2)}, u32[]{:S(2)}) async-start(s32[16,18,1]{1,2,0:T(1,128)} %bitcast), calls=%async_computation | async-start | bytes 16384 | tf_op jit(solution)/shard_map/all_to_all | solution.py:32
  18.1 1.6 scatter_custom_fusion.1
  19.8 1.1 all_to_all.19
  20.8 4.8 %all-to-all-done = s32[16,18,1]{1,2,0:T(1,128)S(1)} async-done(((s32[16,18,1]{1,2,0:T(1,128)}), s32[16,18,1]{1,2,0:T(1,128)S(1)}, u32[]{:S(2)}, u32[]{:S(2)}) %all-to-all-start) | async-done | bytes 1184 | tf_op jit(solution)/shard_map/all_to_all | solution.py:32
  25.6 3.6 all-to-all-start.1
  29.2 0.0 all-gather.5.cloned.1.call-start
  29.3 0.5 broadcast.71
  29.8 0.7 reduce.5
  30.5 0.1 all_to_all.18
  30.6 11.8 %all-to-all-done.1 = bf16[16,18,1024]{2,1,0:T(8,128)(2,1)S(1)} async-done(((bf16[16,18,1024]{2,1,0:T(8,128)(2,1)}), bf16[16,18,1024]{2,1,0:T(8,128)(2,1)S(1)}, u32[]{:S(2)}, u32[]{:S(2)}) %all-to-all-start.1) | async-done | bytes 589856 | tf_op jit(solution)/shard_map/all_to_all | solution.py:31
  42.4 0.2 reshape.67
  42.6 2.4 scatter_custom_fusion.2
  45.0 0.0 all-gather.5.cloned.1.call-update
  45.0 0.0 all-gather.9.cloned.1.call-start
  45.1 0.1 select_reduce_fusion.2
  45.2 36.8 %psum.7 = f32[8]{0:T(128)S(1)} all-reduce(f32[8]{0:T(128)S(1)} %select_reduce_fusion.2), channel_id=1, replica_groups=mesh['row'=8,'col'=16] {'col'}, use_global_device_ids=true, to_apply=%region_8.9 | all-reduce | flops 8 | bytes 64 | tf_op jit(solution)/shard_map/psum | solution.py:61
  82.0 0.1 slice.20
  82.1 0.1 slice.21
  82.2 0.1 copy.18
  82.3 0.1 mul.75
  82.4 0.1 select_reduce_fusion.1
  82.5 0.8 multiply_convert_fusion.1
  83.3 0.0 all-gather.9.cloned.1.call-update
  83.3 0.0 reduce-scatter.5.cloned.1.call-start
  83.4 0.0 copy-start.1
  83.4 3.0 constant_dynamic-update-slice_fusion.1
  86.4 1.4 constant_dynamic-update-slice_fusion
  87.8 3.2 all-gather.5.cloned.1.call-done
  90.9 10.1 %convolution_convert_fusion = bf16[1536,1792]{1,0:T(8,128)(2,1)} fusion(bf16[1536,1024]{1,0:T(8,128)(2,1)} %all-gather.5.cloned.1.call-done, bf16[1024,1792]{1,0:T(8,128)(2,1)} %constant_dynamic-update-slice_fusion), kind=kOutput, calls=%fused_computation.3 | convolution fusion | flops 5639897088 | bytes 12320768 | tf_op jit(solution)/shard_map/dot_general | solution.py:42
  101.0 0.0 reduce-scatter.5.cloned.1.call-update
  101.1 0.0 reduce-scatter.9.cloned.1.call-start
  101.1 39.5 %all-gather.9.cloned.1.call-done = bf16[1536,1024]{1,0:T(8,128)(2,1)} async-done(((bf16[96,1024]{1,0:T(8,128)(2,1)}), bf16[1536,1024]{1,0:T(8,128)(2,1)}) %all-gather.9.cloned.1.call-update) | async-done | bytes 3145744 | tf_op jit(solution)/shard_map/all_gather | solution.py:67
  140.6 6.6 %convolution_convert_fusion.3 = bf16[1536,896]{1,0:T(8,128)(2,1)} fusion(bf16[1536,1024]{1,0:T(8,128)(2,1)} %all-gather.9.cloned.1.call-done, bf16[896,1024]{1,0:T(8,128)(2,1)S(1)} %copy-done), kind=kOutput, calls=%fused_computation.6 | convolution fusion | flops 2819948544 | bytes 7733248 | tf_op jit(solution)/shard_map/dot_general | solution.py:70
  147.2 0.0 reduce-scatter.9.cloned.1.call-update
  147.2 0.0 all-gather.7.cloned.1.call-start
  147.3 35.3 %reduce-scatter.5.cloned.1.call-done = bf16[192,1792]{1,0:T(8,128)(2,1)} async-done(((bf16[1536,1792]{1,0:T(8,128)(2,1)}), bf16[192,1792]{1,0:T(8,128)(2,1)}) %reduce-scatter.5.cloned.1.call-update) | async-done | bytes 688144 | tf_op jit(solution)/shard_map/reduce_scatter | solution.py:41
  182.5 1.2 convert_element_type.39
  183.7 36.1 %reduce-scatter.9.cloned.1.call-done = bf16[192,896]{1,0:T(8,128)(2,1)} async-done(((bf16[1536,896]{1,0:T(8,128)(2,1)}), bf16[192,896]{1,0:T(8,128)(2,1)}) %reduce-scatter.9.cloned.1.call-update) | async-done | bytes 344080 | tf_op jit(solution)/shard_map/reduce_scatter | solution.py:69
  219.8 2.2 fusion.2
  222.0 0.0 all-gather.7.cloned.1.call-update
  222.0 0.0 all-gather.11.cloned.1.call-start
  222.1 1.9 pad_maximum_fusion
  223.9 0.0 all-gather.11.cloned.1.call-update
  224.0 0.0 reduce-scatter.7.cloned.1.call-start
  224.0 23.4 %all-gather.7.cloned.1.call-done = bf16[1536,896]{1,0:T(8,128)(2,1)} async-done(((bf16[192,896]{1,0:T(8,128)(2,1)}), bf16[1536,896]{1,0:T(8,128)(2,1)}) %all-gather.7.cloned.1.call-update) | async-done | bytes 2752528 | tf_op jit(solution)/shard_map/all_gather | solution.py:50
  247.4 6.6 %convolution_convert_fusion.2 = bf16[1536,1024]{1,0:T(8,128)(2,1)} fusion(bf16[1536,896]{1,0:T(8,128)(2,1)} %all-gather.7.cloned.1.call-done, bf16[896,1024]{1,0:T(8,128)(2,1)S(1)} %copy-done), kind=kOutput, calls=%fused_computation.5 | convolution fusion | flops 2820145152 | bytes 7733248 | tf_op jit(solution)/shard_map/dot_general | solution.py:53
  254.0 0.0 reduce-scatter.7.cloned.1.call-update
  254.1 0.2 reduce-scatter.11.cloned.1.call-start
  254.3 33.5 %all-gather.11.cloned.1.call-done = bf16[1536,1792]{1,0:T(8,128)(2,1)} async-done(((bf16[192,1792]{1,0:T(8,128)(2,1)}), bf16[1536,1792]{1,0:T(8,128)(2,1)}) %all-gather.11.cloned.1.call-update) | async-done | bytes 5505040 | tf_op jit(solution)/shard_map/all_gather | solution.py:81
  287.8 10.5 %convolution_convert_fusion.1 = bf16[1536,1024]{1,0:T(8,128)(2,1)} fusion(bf16[1536,1792]{1,0:T(8,128)(2,1)} %all-gather.11.cloned.1.call-done, bf16[1024,1792]{1,0:T(8,128)(2,1)} %constant_dynamic-update-slice_fusion), kind=kOutput, calls=%fused_computation.4 | convolution fusion | flops 5638717440 | bytes 12320768 | tf_op jit(solution)/shard_map/dot_general | solution.py:92
  298.3 0.0 reduce-scatter.11.cloned.1.call-update
  298.3 0.0 slice-start.1
  298.3 7.8 %fusion.15 = f32[896,1024]{1,0:T(8,128)} fusion(bf16[1536,896]{1,0:T(8,128)(2,1)} %all-gather.7.cloned.1.call-done, bf16[1536,1024]{1,0:T(8,128)(2,1)} %all-gather.9.cloned.1.call-done), kind=kOutput, calls=%fused_computation.42 | convolution fusion | flops 2818572288 | bytes 9568256 | tf_op jit(solution)/shard_map/dot_general | solution.py:82
  306.1 6.0 %fusion.14 = f32[1024,1792]{1,0:T(8,128)S(1)} fusion(bf16[1536,1024]{1,0:T(8,128)(2,1)S(1)} %copy-done.3, bf16[1536,1792]{1,0:T(8,128)(2,1)S(1)} %bitcast.19), kind=kOutput, calls=%fused_computation.41 | convolution fusion | flops 5637144576 | bytes 15990784 | tf_op jit(solution)/shard_map/dot_general | solution.py:85
  312.1 3.5 fusion.13
  315.6 52.6 %reduce-scatter.7.cloned.1.call-done = bf16[96,1024]{1,0:T(8,128)(2,1)} async-done(((bf16[1536,1024]{1,0:T(8,128)(2,1)}), bf16[96,1024]{1,0:T(8,128)(2,1)}) %reduce-scatter.7.cloned.1.call-update) | async-done | bytes 196624 | tf_op jit(solution)/shard_map/reduce_scatter | solution.py:52
  368.2 79.4 %reduce-scatter.11.cloned.1.call-done = bf16[96,1024]{1,0:T(8,128)(2,1)} async-done(((bf16[1536,1024]{1,0:T(8,128)(2,1)}), bf16[96,1024]{1,0:T(8,128)(2,1)}) %reduce-scatter.11.cloned.1.call-update) | async-done | bytes 196624 | tf_op jit(solution)/shard_map/reduce_scatter | solution.py:91
  (18 shorter events, 0.1 us)
Async XLA Ops:
  7.2 133.4 %copy-start = (bf16[896,1024]{1,0:T(8,128)(2,1)S(1)}, bf16[896,1024]{1,0:T(8,128)(2,1)}, u32[]{:S(2)}) copy-start(bf16[896,1024]{1,0:T(8,128)(2,1)} %param.12) | copy-start | bytes 5505028
  7.2 37.9 %copy-start.4 = (f32[96]{0:T(128)S(1)}, f32[96]{0:T(128)}, u32[]{:S(2)}) copy-start(f32[96]{0:T(128)} %param.14) | copy-start | bytes 1156
  7.2 37.9 %copy-start.5 = (s32[96]{0:T(128)S(1)}, s32[96]{0:T(128)}, u32[]{:S(2)}) copy-start(s32[96]{0:T(128)} %param.13) | copy-start | bytes 1156
  7.2 75.3 %copy-start.2 = (bf16[96,1024]{1,0:T(8,128)(2,1)S(1)}, bf16[96,1024]{1,0:T(8,128)(2,1)}, u32[]{:S(2)}) copy-start(bf16[96,1024]{1,0:T(8,128)(2,1)} %param.15) | copy-start | bytes 589828
  10.0 15.6 %all-to-all-start = ((s32[16,18,1]{1,2,0:T(1,128)}), s32[16,18,1]{1,2,0:T(1,128)S(1)}, u32[]{:S(2)}, u32[]{:S(2)}) async-start(s32[16,18,1]{1,2,0:T(1,128)} %bitcast), calls=%async_computation | async-start | bytes 16384 | tf_op jit(solution)/shard_map/all_to_all | solution.py:32
  25.6 16.8 %all-to-all-start.1 = ((bf16[16,18,1024]{2,1,0:T(8,128)(2,1)}), bf16[16,18,1024]{2,1,0:T(8,128)(2,1)S(1)}, u32[]{:S(2)}, u32[]{:S(2)}) async-start(bf16[16,18,1024]{2,1,0:T(8,128)(2,1)} %all_to_all.19), calls=%async_computation.1 | async-start | bytes 1572864 | tf_op jit(solution)/shard_map/all_to_all | solution.py:31
  29.2 61.7 %all-gather.5.cloned.1.call-start = ((), (), s32[]{:S(2)}) async-start(), calls=%async_computation.6 | async-start | bytes 3342336 | tf_op jit(solution)/shard_map/all_gather | solution.py:35
  45.0 95.5 %all-gather.9.cloned.1.call-start = ((), (), s32[]{:S(2)}) async-start(), calls=%async_computation.10 | async-start | bytes 3342336 | tf_op jit(solution)/shard_map/all_gather | solution.py:67
  83.3 99.2 %reduce-scatter.5.cloned.1.call-start = ((), (), s32[]{:S(2)}) async-start(), calls=%async_computation.7 | async-start | bytes 6193152 | tf_op jit(solution)/shard_map/reduce_scatter | solution.py:41
  83.4 3.0 copy-start.1
  101.1 118.7 %reduce-scatter.9.cloned.1.call-start = ((), (), s32[]{:S(2)}) async-start(), calls=%async_computation.11 | async-start | bytes 3096576 | tf_op jit(solution)/shard_map/reduce_scatter | solution.py:69
  147.2 100.2 %all-gather.7.cloned.1.call-start = ((), (), s32[]{:S(2)}) async-start(), calls=%async_computation.8 | async-start | bytes 3096576 | tf_op jit(solution)/shard_map/all_gather | solution.py:50
  222.0 65.8 %all-gather.11.cloned.1.call-start = ((), (), s32[]{:S(2)}) async-start(), calls=%async_computation.12 | async-start | bytes 6193152 | tf_op jit(solution)/shard_map/all_gather | solution.py:81
  224.0 144.2 %reduce-scatter.7.cloned.1.call-start = ((), (), s32[]{:S(2)}) async-start(), calls=%async_computation.9 | async-start | bytes 3342336 | tf_op jit(solution)/shard_map/reduce_scatter | solution.py:52
  254.1 193.5 %reduce-scatter.11.cloned.1.call-start = ((), (), s32[]{:S(2)}) async-start(), calls=%async_computation.13 | async-start | bytes 3342336 | tf_op jit(solution)/shard_map/reduce_scatter | solution.py:91
  298.3 7.8 %slice-start = ((s8[5505024]{0:T(1024)(128)(4,1)}), s8[1310720]{0:T(1024)(128)(4,1)S(1)}, s32[]{:S(2)}) async-start(s8[5505024]{0:T(1024)(128)(4,1)} %bitcast.18), calls=%async_computation.14 | async-start | bytes 2621440
  298.3 7.8 %slice-start.1 = ((s8[5505024]{0:T(1024)(128)(4,1)}), s8[4194304]{0:T(1024)(128)(4,1)S(1)}, s32[]{:S(2)}) async-start(s8[5505024]{0:T(1024)(128)(4,1)} %bitcast.18), calls=%async_computation.15 | async-start | bytes 8388608
  298.3 7.8 %copy-start.3 = (bf16[1536,1024]{1,0:T(8,128)(2,1)S(1)}, bf16[1536,1024]{1,0:T(8,128)(2,1)}, u32[]{:S(2)}) copy-start(bf16[1536,1024]{1,0:T(8,128)(2,1)} %all-gather.5.cloned.1.call-done) | copy-start | bytes 9437188
Sparse Core Ops, SparseCore 0:
  45.2 45.7 all-gather.4
  93.7 46.8 all-gather.8
  143.0 39.4 reduce-scatter.4
  185.4 34.3 reduce-scatter.8
  222.1 25.2 all-gather.6
  249.7 38.1 all-gather.10
  292.1 76.0 reduce-scatter.6
  372.5 75.0 reduce-scatter.10
where the time goes:
time: 455 us; the launch traced here: 454 us
  waiting for transfers between devices  320 us (70%)
  matrix products  47.5 us (10%)
  blocking collectives  36.8 us (8%)
  local copies, waits for them, and re-layouts  15.7 us (3%)
  between operations  14.3 us (3%)
  starting transfers between devices  12.3 us (3%)
  other arithmetic  8.19 us (2%)
    reduce_scatter x1, waiting for transfers between devices, per_device(): lax.psum_scatter(lax.dot_general(row_block, both_weights, contract_last,...  79.4 us
    reduce_scatter x1, waiting for transfers between devices, per_device(): lax.psum_scatter(jnp.dot(row_block, down_weight, preferred_element_type=j...  52.6 us
    all_gather x1, waiting for transfers between devices, per_device(): grads_all = lax.all_gather(out_grad, 'col', axis=0, tiled=True)  39.5 us
    psum x1, blocking collectives, per_device(): totals = lax.psum(jnp.sum(log_ratio[:, None] * member, 0), 'col')  36.8 us
    reduce_scatter x1, waiting for transfers between devices, per_device(): lax.psum_scatter(lax.dot_general(row_block, down_weight, contract_last, p...  36.1 us
    reduce_scatter x1, waiting for transfers between devices, per_device(): lax.psum_scatter(jnp.dot(row_block, both_weights, preferred_element_type=...  35.3 us
    all_gather x1, waiting for transfers between devices, per_device(): act_all = lax.all_gather(act_share, 'row', axis=0, tiled=True)  33.5 us
    all_gather x1, waiting for transfers between devices, per_device(): hidden_all = lax.all_gather(hidden_share, 'row', axis=0, tiled=True)  23.4 us
  transfers between devices with their start and end apart: 10, of which 10 were waited for; matrix products, arithmetic and copies ran while one was open for 14% of the time, Pallas kernels for 0%

commit v1 on v0

v1 whole, which is shorter than its diff:
```python
import jax
import jax.numpy as jnp
from jax import lax
from jax.experimental import pallas as pl
from jax.experimental.pallas import tpu as pltpu
from jax.sharding import PartitionSpec as P

BETA = 0.1
F32, BF16 = jnp.float32, jnp.bfloat16
TOK, DB, FB = 1536, 1024, 896
BLOCK, HALF = 96, 48
CHUNK, SHARE = 384, 48
PLANE = 192
PLANE_OFF = (2, 1, -1, 0)
MINOR_OFF = (0, 1, -1, 2)
KINDS = dict(pre=2 * FB, gh=FB)
NT = (((0,), (0,)), ((), ()))
TN = (((1,), (1,)), ((), ()))


def rows(start, size):
    return pl.ds(start, size)


def kernel(info, loaded, token_grad, gw, uw, dw, mixed, ginp, ggate, gup, gdown, *scratch):
    (tiles, weights, down, xl, xs, grads, pre, pre_pair, pre_r1, pre_r2, pre_share, hid, ghp, gh_pair,
     gh_r1, gh_r2, act, part_m, part_i, c1, c2, c3, onehot, places, stage, stage_d, send, recv, local) = scratch
    row, col = lax.axis_index("row"), lax.axis_index("col")
    x, k, z, y = row // 2, row % 2, col // 4, col % 4

    def device(dx=0, dk=0, dz=0, dy=0):
        return {
            "row": lax.rem(x + dx + 4, 4) * 2 + lax.rem(k + dk, 2),
            "col": lax.rem(z + dz + 4, 4) * 4 + lax.rem(y + dy + 4, 4),
        }

    sent = []

    def transfer(src, dst, target, landing=None):
        index = len(sent)
        copy = pltpu.make_async_remote_copy(
            src_ref=src, dst_ref=dst, send_sem=send.at[index], recv_sem=recv.at[index],
            device_id=target, device_id_type=pl.DeviceIdType.MESH,
        )
        copy.start()
        sent.append(copy)
        if landing is None:
            return copy
        return pltpu.make_async_remote_copy(
            src_ref=src, dst_ref=landing, send_sem=send.at[index], recv_sem=recv.at[index],
            device_id=target, device_id_type=pl.DeviceIdType.MESH,
        )

    local_copies = []

    def fetch(src, dst):
        copy = pltpu.make_async_copy(src, dst, local.at[len(local_copies)])
        copy.start()
        local_copies.append(copy)
        return copy

    weight_copies = [fetch(gw, weights.at[:, 0:FB]), fetch(uw, weights.at[:, FB : 2 * FB]), fetch(dw, down)]

    others = [(dz, dy) for dz in range(4) for dy in range(4) if (dz, dy) != (0, 0)]
    barrier = pltpu.get_barrier_semaphore()
    peers = [device(dz=dz, dy=dy) for dz, dy in others]
    peers += [device(dx=1), device(dx=-1), device(dk=1)]
    for peer in peers:
        pl.semaphore_signal(barrier, inc=1, device_id=peer, device_id_type=pl.DeviceIdType.MESH)
    pl.semaphore_wait(barrier, len(peers))

    def along(half, major=0, minor=0):
        return device(dz=major, dy=minor) if half == 0 else device(dz=minor, dy=major)

    def place(half, plane, minor):
        return rows(half * 768 + plane * PLANE + minor * HALF, HALF)

    class Gather:
        def __init__(self, buf):
            self.buf, self.got = buf, {}

        def move(self, half, src, dst, target):
            self.got[(half,) + dst] = transfer(
                self.buf.at[place(half, *src)], self.buf.at[place(half, *dst)], target
            )

        def spread(self, half, minor):
            self.move(half, (3, minor), (2, minor), along(half, major=1))
            self.move(half, (3, minor), (1, minor), along(half, major=-1))

        def begin(self):
            for half in (0, 1):
                self.move(half, (3, 0), (3, 2), along(half, minor=1))
                self.move(half, (3, 0), (3, 1), along(half, minor=-1))
                self.move(half, (3, 0), (3, 3), along(half, minor=2))
                self.spread(half, 0)

        def wait(self, half, plane, minor):
            self.got[(half, plane, minor)].wait_recv()

        def first(self):
            for minor in (1, 2):
                for half in (0, 1):
                    self.wait(half, 3, minor)
                    self.spread(half, minor)
            for half in (0, 1):
                self.wait(half, 3, 3)
                self.spread(half, 3)

        def second(self):
            for half in (0, 1):
                self.wait(half, 2, 0)
                self.move(half, (2, 0), (0, 0), along(half, major=1))
            for half in (0, 1):
                self.wait(half, 2, 1)
                self.move(half, (2, 1), (0, 1), along(half, major=1))
            for half in (0, 1):
                self.wait(half, 1, 2)
                self.move(half, (1, 2), (0, 2), along(half, major=-1))
            for half in (0, 1):
                self.wait(half, 1, 3)
                self.move(half, (1, 3), (0, 3), along(half, major=-1))

        def finish(self):
            for half in (0, 1):
                for plane, minor in ((1, 0), (1, 1), (2, 2), (2, 3), (0, 0), (0, 1), (0, 2), (0, 3)):
                    self.wait(half, plane, minor)

    gather_x, gather_g = Gather(xl), Gather(grads)
    for half in (0, 1):
        xl[place(half, 3, 0), :] = loaded[rows(half * HALF, HALF), :]
    tiles[0:8, :] = info[...]
    gather_x.begin()
    tile_copies = []
    for dz, dy in others:
        slot = ((-dz) % 4) * 4 + (-dy) % 4
        tile_copies.append(
            transfer(tiles.at[0:8, :], tiles.at[slot * 8 : slot * 8 + 8, :], device(dz=dz, dy=dy))
        )
    gather_x.first()

    for copy in tile_copies:
        copy.wait_recv()
    table = tiles[...]
    turned = table.T

    def slot_of(half, plane, minor):
        major, less = PLANE_OFF[plane] % 4, MINOR_OFF[minor] % 4
        return major * 4 + less if half == 0 else less * 4 + major

    for half in (0, 1):
        for plane in range(4):
            for minor in range(4):
                lane = slot_of(half, plane, minor) * 8
                column = turned[half * HALF : half * HALF + HALF, lane : lane + 1]
                places[place(half, plane, minor), :] = jnp.broadcast_to(column, (HALF, 128)).astype(jnp.int32)
    kind = lax.broadcasted_iota(jnp.int32, (128, 128), 0) % 8
    segment_part = jnp.concatenate([table[8 * i + 1 : 8 * i + 2, :] for i in range(16)], 0)
    ratio_part = jnp.concatenate([table[8 * i + 2 : 8 * i + 3, :] for i in range(16)], 0)
    del kind

    def total(s):
        return jnp.sum(jnp.where(segment_part == float(s), ratio_part, 0.0), axis=(0, 1), keepdims=True)

    own_segment = turned[0:BLOCK, 1:2]
    token_weight = jnp.zeros((BLOCK, 1), F32)
    for p in range(4):
        margin = BETA * (total(2 * p) - total(2 * p + 1))
        pair_weight = -BETA * jax.nn.sigmoid(-margin)
        token_weight = jnp.where(own_segment == float(2 * p), pair_weight, token_weight)
        token_weight = jnp.where(own_segment == float(2 * p + 1), -pair_weight, token_weight)
    for half in (0, 1):
        part = rows(half * HALF, HALF)
        weight = token_weight[half * HALF : half * HALF + HALF, :]
        grads[place(half, 3, 0), :] = (weight * token_grad[part, :].astype(F32)).astype(BF16)
    gather_x.second()
    gather_x.finish()
    gather_g.begin()
    for copy in weight_copies:
        copy.wait()

    def permute(c):
        lane = lax.broadcasted_iota(jnp.int32, (1, CHUNK), 1)
        token = lane
        for j in range(8):
            half, plane, minor = c // 2, (c % 2) * 2 + j // 4, j % 4
            major, less = PLANE_OFF[plane], MINOR_OFF[minor]
            dz, dy = (major, less) if half == 0 else (less, major)
            block = lax.rem(z + dz + 4, 4) * 4 + lax.rem(y + dy + 4, 4)
            inside = (lane >= j * HALF) & (lane < (j + 1) * HALF)
            token = token + jnp.where(inside, block * BLOCK + half * HALF - j * HALF, 0)

        def build(i, carry):
            part = rows(pl.multiple_of(i * 128, 128), 128)
            match = places[part, 0:1] == token
            onehot[part, :] = jnp.where(match, 1.0, 0.0).astype(BF16)
            return carry

        lax.fori_loop(0, TOK // 128, build, 0)
        chunk = rows(c * CHUNK, CHUNK)
        xs[chunk, :] = lax.dot_general(onehot[...], xl[...], NT, preferred_element_type=F32).astype(BF16)

    def pre_matmul(c):
        chunk = rows(c * CHUNK, CHUNK)

        def tile(i, carry):
            cols = rows(pl.multiple_of(i * 256, 256), 256)
            pre[chunk, cols] = jnp.dot(xs[chunk, :], weights[:, cols], preferred_element_type=F32).astype(BF16)
            return carry

        lax.fori_loop(0, 7, tile, 0)

    def gh_matmul(c):
        chunk = rows(c * CHUNK, CHUNK)
        ghp[chunk, :] = lax.dot_general(grads[chunk, :], down[...], TN, preferred_element_type=F32).astype(BF16)

    def mixed_matmul(c):
        chunk = rows(c * CHUNK, CHUNK)

        def tile(i, carry):
            cols = rows(pl.multiple_of(i * 256, 256), 256)
            part_m[chunk, cols] = jnp.dot(hid[chunk, :], down[:, cols], preferred_element_type=F32).astype(BF16)
            return carry

        lax.fori_loop(0, 4, tile, 0)

    def ginp_matmul(c):
        chunk = rows(c * CHUNK, CHUNK)

        def tile(i, carry):
            cols = rows(pl.multiple_of(i * 256, 256), 256)
            part_i[chunk, cols] = lax.dot_general(
                act[chunk, :], weights[cols, :], TN, preferred_element_type=F32
            ).astype(BF16)
            return carry

        lax.fori_loop(0, 4, tile, 0)

    xp, xm, xo = lax.rem(x + 1, 4), lax.rem(x + 3, 4), lax.rem(x + 2, 4)

    class RowChunk:
        def __init__(self, c, part, pair, r1, r2, width, out, out_width):
            self.c, self.part, self.pair, self.r1, self.r2 = c, part, pair, r1, r2
            self.width, self.out, self.out_width = width, out, out_width

        def cut(self, width):
            if width == 2 * FB:
                return FB
            return 512 if self.c % 2 == 0 else 384

        def mine(self, xx):
            return rows(pl.multiple_of(self.c * CHUNK + k * PLANE + xx * SHARE, 16), SHARE)

        def pair_send(self):
            theirs = rows(pl.multiple_of(self.c * CHUNK + (1 - k) * PLANE, 16), PLANE)
            self.pair_copy = transfer(self.part.at[theirs, :], self.pair.at[self.c], device(dk=1))

        def pair_add(self):
            self.pair_copy.wait_recv()
            mine = rows(pl.multiple_of(self.c * CHUNK + k * PLANE, 16), PLANE)
            both = self.part[mine, :].astype(F32) + self.pair[self.c].astype(F32)
            self.part[mine, :] = both.astype(BF16)
            cut, far = self.cut(self.width), self.mine(xo)
            self.far = [
                transfer(self.part.at[far, 0:cut], self.r1.at[self.c, :, 0:cut], device(dx=1)),
                transfer(self.part.at[far, cut : self.width], self.r1.at[self.c, :, cut : self.width], device(dx=-1)),
            ]

        def ring_add(self):
            cut = self.cut(self.width)
            self.near = []
            for i, (xx, lo, hi, dx) in enumerate(((xp, 0, cut, 1), (xm, cut, self.width, -1))):
                self.far[i].wait_recv()
                mine = self.mine(xx)
                both = self.part[mine, lo:hi].astype(F32) + self.r1[self.c, :, lo:hi].astype(F32)
                self.part[mine, lo:hi] = both.astype(BF16)
                self.near.append(transfer(self.part.at[mine, :], self.r2.at[self.c, i], device(dx=dx)))

        def total(self):
            self.near[0].wait_recv()
            self.near[1].wait_recv()
            return (
                self.part[self.mine(x), :].astype(F32)
                + self.r2[self.c, 0].astype(F32)
                + self.r2[self.c, 1].astype(F32)
            )

        def out_send(self):
            own = self.out.at[self.mine(x), :]
            self.side = [
                transfer(own, own, device(dx=1), self.out.at[self.mine(xm), :]),
                transfer(own, own, device(dx=-1), self.out.at[self.mine(xp), :]),
            ]

        def out_forward(self):
            cut = self.cut(self.out_width)
            self.last = []
            for i, (xx, lo, hi, dx) in enumerate(((xm, 0, cut, 1), (xp, cut, self.out_width, -1))):
                self.side[i].wait_recv()
                piece = self.out.at[self.mine(xx), lo:hi]
                self.last.append(transfer(piece, piece, device(dx=dx), self.out.at[self.mine(xo), lo:hi]))

        def out_pair(self):
            self.last[0].wait_recv()
            self.last[1].wait_recv()
            mine = self.out.at[rows(pl.multiple_of(self.c * CHUNK + k * PLANE, 16), PLANE), :]
            theirs = self.out.at[rows(pl.multiple_of(self.c * CHUNK + (1 - k) * PLANE, 16), PLANE), :]
            self.done = transfer(mine, mine, device(dk=1), theirs)

        def out_wait(self):
            self.done.wait_recv()

    forward = [RowChunk(c, pre, pre_pair, pre_r1, pre_r2, 2 * FB, hid, FB) for c in range(4)]
    backward = [RowChunk(c, ghp, gh_pair, gh_r1, gh_r2, FB, act, 2 * FB) for c in range(4)]

    def hidden(c):
        both = forward[c].total()
        pre_share[c] = both
        gate, up = both[:, :FB], both[:, FB:]
        hid[forward[c].mine(x), :] = (gate * jax.nn.sigmoid(gate) * up).astype(BF16)
        forward[c].out_send()

    def acts(c):
        grad = backward[c].total()
        gate, up = pre_share[c, :, 0:FB], pre_share[c, :, FB : 2 * FB]
        s = jax.nn.sigmoid(gate)
        mine = backward[c].mine(x)
        act[mine, 0:FB] = (grad * up * s * (1.0 + gate * (1.0 - s))).astype(BF16)
        act[mine, FB : 2 * FB] = (grad * gate * s).astype(BF16)
        backward[c].out_send()

    class ColSum:
        def __init__(self, half, which, part, out):
            self.half, self.part, self.out = half, part, out
            self.c1, self.c2, self.c3 = c1.at[which], c2.at[which], c3.at[which]

        def plane(self, p):
            return self.half * 768 + p * PLANE

        def send_far(self):
            start = self.plane(0)
            self.far = [
                transfer(self.part.at[rows(start, 96), :], self.c1.at[0], along(self.half, major=1)),
                transfer(self.part.at[rows(start + 96, 96), :], self.c1.at[1], along(self.half, major=-1)),
            ]
            self.near = [None, None]

        def send_near(self, i):
            self.far[i].wait_recv()
            start = self.plane(1 + i)
            mine = rows(start + i * 96, 96)
            self.part[mine, :] = (self.part[mine, :].astype(F32) + self.c1[i].astype(F32)).astype(BF16)
            self.near[i] = transfer(
                self.part.at[rows(start, PLANE), :], self.c2.at[i], along(self.half, major=1 if i == 0 else -1)
            )

        def send_minor(self):
            self.near[0].wait_recv()
            self.near[1].wait_recv()
            own = rows(self.plane(3), PLANE)
            self.part[own, :] = (
                self.part[own, :].astype(F32) + self.c2[0].astype(F32) + self.c2[1].astype(F32)
            ).astype(BF16)
            self.minor = []
            for m in (1, 2, 3):
                self.minor.append(
                    transfer(
                        self.part.at[rows(self.plane(3) + m * HALF, HALF), :],
                        self.c3.at[m - 1],
                        along(self.half, minor=MINOR_OFF[m]),
                    )
                )

        def store(self):
            total = self.part[rows(self.plane(3), HALF), :].astype(F32)
            for i in range(3):
                self.minor[i].wait_recv()
                total = total + self.c3[i].astype(F32)
            self.out[rows(self.half * HALF, HALF), :] = total.astype(BF16)

    mixed_sum = [ColSum(h, h, part_m, mixed) for h in (0, 1)]
    ginp_sum = [ColSum(h, 2 + h, part_i, ginp) for h in (0, 1)]

    flush = {}

    def push(key, stage_ref, out_ref, value):
        if key in flush:
            flush[key].wait()
        stage_ref[...] = value
        flush[key] = fetch(stage_ref, out_ref)

    def down_grad(i):
        cols = rows(i * 256, 256)
        push(("d", i % 2), stage_d.at[i % 2], gdown.at[:, cols],
             lax.dot_general(hid[...], grads[:, cols], NT, preferred_element_type=F32))

    def up_grad(i):
        which, j = i // 4, i % 4
        cols = rows(j * 256, 256)
        target = (ggate, gup)[which]
        push(("u", i % 2), stage.at[i % 2], target.at[cols, :],
             lax.dot_general(xs[:, cols], act[:, which * FB : (which + 1) * FB], NT, preferred_element_type=F32))

    def step_pre(c):
        permute(c)
        pre_matmul(c)
        forward[c].pair_send()

    def step_gh(c):
        gh_matmul(c)
        backward[c].pair_send()

    step_pre(0)
    gather_g.first()
    step_pre(1)
    forward[0].pair_add()
    gather_g.second()
    step_pre(2)
    forward[0].ring_add()
    forward[1].pair_add()
    step_pre(3)
    hidden(0)
    forward[1].ring_add()
    forward[2].pair_add()
    gather_g.finish()
    step_gh(0)
    forward[0].out_forward()
    hidden(1)
    forward[2].ring_add()
    forward[3].pair_add()
    backward[0].pair_add()
    step_gh(1)
    forward[0].out_pair()
    forward[1].out_forward()
    hidden(2)
    forward[3].ring_add()
    backward[0].ring_add()
    backward[1].pair_add()
    step_gh(2)
    forward[0].out_wait()
    mixed_matmul(0)
    mixed_sum[0].send_far()
    forward[1].out_pair()
    forward[2].out_forward()
    hidden(3)
    acts(0)
    backward[1].ring_add()
    backward[2].pair_add()
    step_gh(3)
    forward[1].out_wait()
    mixed_matmul(1)
    mixed_sum[0].send_near(0)
    mixed_sum[0].send_near(1)
    forward[2].out_pair()
    forward[3].out_forward()
    backward[0].out_forward()
    acts(1)
    backward[2].ring_add()
    backward[3].pair_add()
    forward[2].out_wait()
    mixed_matmul(2)
    mixed_sum[1].send_far()
    forward[3].out_pair()
    backward[0].out_pair()
    backward[1].out_forward()
    acts(2)
    backward[3].ring_add()
    mixed_sum[0].send_minor()
    forward[3].out_wait()
    mixed_matmul(3)
    mixed_sum[1].send_near(0)
    mixed_sum[1].send_near(1)
    backward[0].out_wait()
    ginp_matmul(0)
    ginp_sum[0].send_far()
    backward[1].out_pair()
    backward[2].out_forward()
    acts(3)
    mixed_sum[0].store()
    down_grad(0)
    backward[1].out_wait()
    ginp_matmul(1)
    ginp_sum[0].send_near(0)
    ginp_sum[0].send_near(1)
    mixed_sum[1].send_minor()
    backward[2].out_pair()
    backward[3].out_forward()
    down_grad(1)
    backward[2].out_wait()
    ginp_matmul(2)
    ginp_sum[1].send_far()
    backward[3].out_pair()
    ginp_sum[0].send_minor()
    mixed_sum[1].store()
    down_grad(2)
    backward[3].out_wait()
    ginp_matmul(3)
    ginp_sum[1].send_near(0)
    ginp_sum[1].send_near(1)
    down_grad(3)
    for i in range(5):
        up_grad(i)
    ginp_sum[0].store()
    ginp_sum[1].send_minor()
    for i in range(5, 8):
        up_grad(i)
    ginp_sum[1].store()
    for copy in flush.values():
        copy.wait()
    for copy in sent:
        copy.wait_send()


def per_device(loaded, positions, gate_weight, up_weight, down_weight, segment, log_ratio, token_grad):
    info = jnp.stack([positions.astype(F32), segment.astype(F32), log_ratio], 0)
    info = jnp.pad(info, ((0, 5), (0, 128 - BLOCK)), constant_values=-1.0)
    vmem, anywhere = pl.BlockSpec(memory_space=pltpu.VMEM), pl.BlockSpec(memory_space=pl.ANY)
    shape = jax.ShapeDtypeStruct
    buf = lambda *s: pltpu.VMEM(s, BF16)
    transfers = 200
    scratch = [
        pltpu.VMEM((128, 128), F32),
        buf(DB, 2 * FB),
        buf(FB, DB),
        buf(TOK, DB),
        buf(TOK, DB),
        buf(TOK, DB),
        buf(TOK, 2 * FB),
        buf(4, PLANE, 2 * FB),
        buf(4, SHARE, 2 * FB),
        buf(4, 2, SHARE, 2 * FB),
        pltpu.VMEM((4, SHARE, 2 * FB), F32),
        buf(TOK, FB),
        buf(TOK, FB),
        buf(4, PLANE, FB),
        buf(4, SHARE, FB),
        buf(4, 2, SHARE, FB),
        buf(TOK, 2 * FB),
        buf(TOK, DB),
        buf(TOK, DB),
        buf(4, 2, 96, DB),
        buf(4, 2, PLANE, DB),
        buf(4, 3, HALF, DB),
        buf(TOK, CHUNK),
        pltpu.VMEM((TOK, 128), jnp.int32),
        pltpu.VMEM((2, 256, FB), F32),
        pltpu.VMEM((2, FB, 256), F32),
        pltpu.SemaphoreType.DMA((transfers,)),
        pltpu.SemaphoreType.DMA((transfers,)),
        pltpu.SemaphoreType.DMA((16,)),
    ]
    return pl.pallas_call(
        kernel,
        out_shape=(
            shape((BLOCK, DB), BF16),
            shape((BLOCK, DB), BF16),
            shape((DB, FB), F32),
            shape((DB, FB), F32),
            shape((FB, DB), F32),
        ),
        in_specs=[vmem] * 3 + [anywhere] * 3,
        out_specs=[vmem] * 2 + [anywhere] * 3,
        scratch_shapes=scratch,
        compiler_params=pltpu.CompilerParams(
            collective_id=0, has_side_effects=True, vmem_limit_bytes=64 * 1024 * 1024
        ),
        name="feed_forward",
    )(info, loaded, token_grad, gate_weight, up_weight, down_weight)


def solution(mesh):
    return jax.shard_map(
        per_device,
        mesh=mesh,
        in_specs=(
            P("col", "row"),
            P("col"),
            P("row", "col"),
            P("row", "col"),
            P("col", "row"),
            P("col"),
            P("col"),
            P("col", "row"),
        ),
        out_specs=(
            P("col", "row"),
            P("col", "row"),
            P("row", "col"),
            P("row", "col"),
            P("col", "row"),
        ),
        check_vma=False,
    )
```

time: 455 us -> 166 us (0.36)
  waiting for transfers between devices: 320 us -> 0 us
  Pallas kernels: 0 us -> 150 us
  matrix products: 47.5 us -> 0 us
  blocking collectives: 36.8 us -> 0 us
  between operations: 14.3 us -> 0.65 us
  starting transfers between devices: 12.3 us -> 0 us
  other arithmetic: 8.19 us -> 1.93 us
    reduce_scatter x4 -> x0, waiting for transfers between devices: 203 us -> none  [the longest x1 79.4 us: per_device(): lax.psum_scatter(lax.dot_general(row_block, both_weights, contract_last,...]
    pallas_call x0 -> x1, Pallas kernels: none -> 150 us  [per_device(): pl.pallas_call(kernel, out_shape=(shape((BLOCK, DB), BF16), shape((BLOCK,...]
    all_gather x4 -> x0, waiting for transfers between devices: 99.6 us -> none  [the longest x1 39.5 us: per_device(): grads_all = lax.all_gather(out_grad, 'col', axis=0, tiled=True)]
    dot_general x6 -> x0, matrix products: 47.5 us -> none  [the longest x1 10.5 us: per_device(): lax.dot_general(row_block, both_weights, contract_last, preferred_element...]
    psum x1 -> x0, blocking collectives: 36.8 us -> none  [per_device(): totals = lax.psum(jnp.sum(log_ratio[:, None] * member, 0), 'col')]
    all_to_all x2 -> x0, waiting for transfers between devices: 16.7 us -> none  [the longest x1 11.8 us: per_device(): lax.all_to_all(send_rows, 'col', split_axis=0, concat_axis=0, tiled=True)]
    all_to_all x2 -> x0, starting transfers between devices: 11.7 us -> none  [the longest x1 8.13 us: per_device(): lax.all_to_all(send_place, 'col', split_axis=0, concat_axis=0, tiled=True)]
    unnamed x17 -> x9, local copies, waits for them, and re-layouts: 3.06 us -> 12.7 us
  transfers between devices with their start and end apart: 10 -> 0, of which waited for: 10 -> 0; matrix products, arithmetic and copies ran while one was open for 14% -> 0% of each run, Pallas kernels for 0% -> 0%
where the time goes in v1:
time: 166 us
  Pallas kernels  150 us (90%)
  local copies, waits for them, and re-layouts  12.7 us (8%)
  other arithmetic  1.93 us (1%)
    pallas_call x1, Pallas kernels, per_device(): pl.pallas_call(kernel, out_shape=(shape((BLOCK, DB), BF16), shape((BLOCK,...  150 us
    unnamed x9, local copies, waits for them, and re-layouts  12.7 us

profile of v1, /device:TPU:0, one launch (start us, length us, event | category | flops | bytes accessed | tf_op | source)
XLA Modules:
  0.0 165.7 jit_solution(12427804959538652468)
XLA Ops:
  0.6 0.7 convert_bitcast_fusion
  1.3 1.3 select_maximum_fusion.info
  2.6 150.4 %feed_forward.1 = (bf16[96,1024]{1,0:T(8,128)(2,1)}, bf16[96,1024]{1,0:T(8,128)(2,1)}, f32[1024,896]{1,0:T(8,128)}, f32[1024,896]{1,0:T(8,128)}, f32[896,1024]{1,0:T(8,128)}) custom-call(f32[8,128]{1,0:T(8,128)} %select_maximum_fusion.info, bf16[96,1024]{1,0:T(8,128)(2,1)} %loaded.1, bf16[96,1024]{1,0:T(8,128)(2,1)} %token_grad.1, bf16[1024,896]{1,0:T(8,128)(2,1)} %gw.1, ...), custom_call_target="tpu_custom_call" | custom-call | tf_op jit(solution)/shard_map/feed_forward/pallas_call | solution.py:552
  153.0 1.6 copy.18
  154.6 1.6 copy.19
  156.2 0.0 copy-start.1
  156.2 4.3 %copy.20 = f32[1024,896]{1,0:T(8,128)} copy(f32[1024,896]{1,0:T(8,128)} %get-tuple-element.14) | data formatting | bytes 7340032
  160.5 0.0 copy-done.1
  160.5 0.0 copy-start
  160.5 1.9 %copy.21 = f32[1024,896]{1,0:T(8,128)} copy(f32[1024,896]{1,0:T(8,128)S(1)} %copy-done.1) | data formatting | bytes 7340032
  162.4 1.5 copy-done
  163.9 1.8 %copy.22 = f32[896,1024]{1,0:T(8,128)} copy(f32[896,1024]{1,0:T(8,128)S(1)} %copy-done) | data formatting | bytes 7340032
Async XLA Ops:
  156.2 4.3 %copy-start.1 = (f32[1024,896]{1,0:T(8,128)S(1)}, f32[1024,896]{1,0:T(8,128)}, u32[]{:S(2)}) copy-start(f32[1024,896]{1,0:T(8,128)} %get-tuple-element.15) | copy-start | bytes 11010052
  160.5 3.4 %copy-start = (f32[896,1024]{1,0:T(8,128)S(1)}, f32[896,1024]{1,0:T(8,128)}, u32[]{:S(2)}) copy-start(f32[896,1024]{1,0:T(8,128)} %get-tuple-element.16) | copy-start | bytes 11010052

commit v2 on v1

v2 whole, which is shorter than its diff:
```python
import jax
import jax.numpy as jnp
from jax import lax
from jax.experimental import pallas as pl
from jax.experimental.pallas import tpu as pltpu
from jax.sharding import PartitionSpec as P

BETA = 0.1
F32, BF16 = jnp.float32, jnp.bfloat16
TOK, DB, FB = 1536, 1024, 896
BLOCK, HALF = 96, 48
CHUNK, SHARE = 384, 48
PLANE = 192
FAR = 384
PLANE_OFF = (2, 1, -1, 0)
MINOR_OFF = (0, 1, -1, 2)
NT = (((0,), (0,)), ((), ()))
TN = (((1,), (1,)), ((), ()))


def rows(start, size):
    return pl.ds(start, size)


def kernel(spots, parts, ratios, loaded, token_grad, gw, uw, dw, mixed, ginp, ggate, gup, gdown, *scratch):
    (tiles, weights, down, xl, xs, grads, pre, pre_pair, pre_r1, pre_r2, pre_share, hid, ghp, gh_pair,
     gh_r1, gh_r2, act, part_m, c1, c2, c3, onehot, onehot_far, places, totals_u, totals_d, send, recv, local) = scratch
    part_i = xl
    row, col = lax.axis_index("row"), lax.axis_index("col")
    x, k, z, y = row // 2, row % 2, col // 4, col % 4

    def device(dx=0, dk=0, dz=0, dy=0):
        return {
            "row": lax.rem(x + dx + 4, 4) * 2 + lax.rem(k + dk, 2),
            "col": lax.rem(z + dz + 4, 4) * 4 + lax.rem(y + dy + 4, 4),
        }

    sent, gone = [], set()

    def transfer(src, dst, target, landing=None):
        index = len(sent)
        copy = pltpu.make_async_remote_copy(
            src_ref=src, dst_ref=dst, send_sem=send.at[index], recv_sem=recv.at[index],
            device_id=target, device_id_type=pl.DeviceIdType.MESH,
        )
        copy.start()
        sent.append(copy)
        if landing is None:
            return copy
        return pltpu.make_async_remote_copy(
            src_ref=src, dst_ref=landing, send_sem=send.at[index], recv_sem=recv.at[index],
            device_id=target, device_id_type=pl.DeviceIdType.MESH,
        )

    local_copies = []

    def fetch(src, dst):
        copy = pltpu.make_async_copy(src, dst, local.at[len(local_copies)])
        copy.start()
        local_copies.append(copy)
        return copy

    weight_copies = [fetch(gw, weights.at[:, 0:FB]), fetch(uw, weights.at[:, FB : 2 * FB]), fetch(dw, down)]

    others = [(dz, dy) for dz in range(4) for dy in range(4) if (dz, dy) != (0, 0)]
    barrier = pltpu.get_barrier_semaphore()
    peers = [device(dz=dz, dy=dy) for dz, dy in others]
    peers += [device(dx=1), device(dx=-1), device(dk=1)]
    for peer in peers:
        pl.semaphore_signal(barrier, inc=1, device_id=peer, device_id_type=pl.DeviceIdType.MESH)
    pl.semaphore_wait(barrier, len(peers))

    def along(half, major=0, minor=0):
        return device(dz=major, dy=minor) if half == 0 else device(dz=minor, dy=major)

    def place(half, plane, minor):
        return rows(plane * CHUNK + half * PLANE + minor * HALF, HALF)

    class Gather:
        def __init__(self, buf):
            self.buf, self.got, self.seen, self.left = buf, {}, set(), False

        def move(self, half, src, dst, target):
            self.got[(half,) + dst] = transfer(
                self.buf.at[place(half, *src)], self.buf.at[place(half, *dst)], target
            )

        def spread(self, half, minor):
            self.move(half, (3, minor), (2, minor), along(half, major=1))
            self.move(half, (3, minor), (1, minor), along(half, major=-1))

        def begin(self):
            for half in (0, 1):
                self.move(half, (3, 0), (3, 2), along(half, minor=1))
                self.move(half, (3, 0), (3, 1), along(half, minor=-1))
                self.move(half, (3, 0), (3, 3), along(half, minor=2))
                self.spread(half, 0)

        def wait(self, half, plane, minor):
            if (half, plane, minor) not in self.seen:
                self.got[(half, plane, minor)].wait_recv()
                self.seen.add((half, plane, minor))

        def spread_on(self, half, minor):
            self.wait(half, 3, minor)
            self.spread(half, minor)

        def forward(self, half, minor):
            plane, way = (2, 1) if minor < 2 else (1, -1)
            self.wait(half, plane, minor)
            self.move(half, (plane, minor), (0, minor), along(half, major=way))

        def need(self, *planes):
            for plane in planes:
                for half in (0, 1):
                    for minor in range(4):
                        if (plane, minor) != (3, 0):
                            self.wait(half, plane, minor)

    gather_x, gather_g = Gather(xl), Gather(grads)
    for half in (0, 1):
        xl[place(half, 3, 0), :] = loaded[rows(half * HALF, HALF), :]
    tiles[0:8, :] = jnp.full((8, 128), -1.0, F32)
    tiles[0:1, 0:BLOCK] = spots[...].astype(F32)
    tiles[1:2, 0:BLOCK] = parts[...].astype(F32)
    tiles[2:3, 0:BLOCK] = ratios[...]
    tile_copies = []

    def send_tiles():
        for dz, dy in others:
            slot = ((-dz) % 4) * 4 + (-dy) % 4
            tile_copies.append(
                transfer(tiles.at[0:8, :], tiles.at[slot * 8 : slot * 8 + 8, :], device(dz=dz, dy=dy))
            )

    def slot_of(half, plane, minor):
        major, less = PLANE_OFF[plane] % 4, MINOR_OFF[minor] % 4
        return major * 4 + less if half == 0 else less * 4 + major

    def tables():
        for copy in tile_copies:
            copy.wait_recv()
        table = tiles[...]
        turned = table.T
        for half in (0, 1):
            for plane in range(4):
                for minor in range(4):
                    lane = slot_of(half, plane, minor) * 8
                    column = turned[half * HALF : half * HALF + HALF, lane : lane + 1]
                    places[place(half, plane, minor), :] = jnp.broadcast_to(column, (HALF, 128)).astype(jnp.int32)
        segment_part = jnp.concatenate([table[8 * i + 1 : 8 * i + 2, :] for i in range(16)], 0)
        ratio_part = jnp.concatenate([table[8 * i + 2 : 8 * i + 3, :] for i in range(16)], 0)

        def total(s):
            return jnp.sum(jnp.where(segment_part == float(s), ratio_part, 0.0), axis=(0, 1), keepdims=True)

        own_segment = turned[0:BLOCK, 1:2]
        token_weight = jnp.zeros((BLOCK, 1), F32)
        for p in range(4):
            margin = BETA * (total(2 * p) - total(2 * p + 1))
            pair_weight = -BETA * jax.nn.sigmoid(-margin)
            token_weight = jnp.where(own_segment == float(2 * p), pair_weight, token_weight)
            token_weight = jnp.where(own_segment == float(2 * p + 1), -pair_weight, token_weight)
        for half in (0, 1):
            part = rows(half * HALF, HALF)
            weight = token_weight[half * HALF : half * HALF + HALF, :]
            grads[place(half, 3, 0), :] = (weight * token_grad[part, :].astype(F32)).astype(BF16)

    ready = []

    def need_weights():
        if not ready:
            for copy in weight_copies:
                copy.wait()
            ready.append(True)

    def tokens_of(c):
        lane = lax.broadcasted_iota(jnp.int32, (1, CHUNK), 1)
        token = lane
        for j in range(8):
            half, minor = j // 4, j % 4
            major, less = PLANE_OFF[c], MINOR_OFF[minor]
            dz, dy = (major, less) if half == 0 else (less, major)
            block = lax.rem(z + dz + 4, 4) * 4 + lax.rem(y + dy + 4, 4)
            inside = (lane >= j * HALF) & (lane < (j + 1) * HALF)
            token = token + jnp.where(inside, block * BLOCK + half * HALF - j * HALF, 0)
        return token

    def match(c, first, count, ref):
        token = tokens_of(c)

        def build(i, carry):
            part = rows(pl.multiple_of(i * 128, 128), 128)
            here = places[rows(pl.multiple_of(first + i * 128, 128), 128), 0:1]
            ref[part, :] = jnp.where(here == token, 1.0, 0.0).astype(BF16)
            return carry

        lax.fori_loop(0, count // 128, build, 0)

    def permute_most(c):
        gather_x.need(1, 2, 3)
        match(c, FAR, TOK - FAR, onehot)
        xs[rows(c * CHUNK, CHUNK), :] = lax.dot_general(
            onehot[...], xl[FAR:TOK, :], NT, preferred_element_type=F32
        ).astype(BF16)

    def permute_rest(c):
        gather_x.need(0)
        match(c, 0, FAR, onehot_far)
        chunk = rows(c * CHUNK, CHUNK)
        rest = lax.dot_general(onehot_far[...], xl[0:FAR, :], NT, preferred_element_type=F32)
        xs[chunk, :] = (xs[chunk, :].astype(F32) + rest).astype(BF16)

    def pre_matmul(c, i):
        need_weights()
        chunk, cols = rows(c * CHUNK, CHUNK), rows(i * FB, FB)
        pre[chunk, cols] = jnp.dot(xs[chunk, :], weights[:, cols], preferred_element_type=F32).astype(BF16)
        forward[c].pair_send(i)

    def gh_matmul(c):
        need_weights()
        gather_g.need(c)
        chunk = rows(c * CHUNK, CHUNK)
        ghp[chunk, :] = lax.dot_general(grads[chunk, :], down[...], TN, preferred_element_type=F32).astype(BF16)
        backward[c].pair_send(0)

    def mixed_matmul(c):
        chunk = rows(c * CHUNK, CHUNK)
        forward[c].out_wait()
        part_m[chunk, :] = jnp.dot(hid[chunk, :], down[...], preferred_element_type=F32).astype(BF16)

    def ginp_matmul(c):
        chunk = rows(c * CHUNK, CHUNK)
        backward[c].out_wait()
        if not gather_x.left:
            gather_x.left = True
            for copy in gather_x.got.values():
                copy.wait_send()
                gone.add(id(copy))
        part_i[chunk, :] = lax.dot_general(
            act[chunk, :], weights[...], TN, preferred_element_type=F32
        ).astype(BF16)

    xp, xm, xo = lax.rem(x + 1, 4), lax.rem(x + 3, 4), lax.rem(x + 2, 4)

    class RowChunk:
        def __init__(self, c, part, pair, r1, r2, width, out, out_width):
            self.c, self.part, self.pair, self.r1, self.r2 = c, part, pair, r1, r2
            self.width, self.out, self.out_width = width, out, out_width
            self.pairs, self.far, self.near, self.last = {}, {}, {}, {}

        def cut(self, width):
            if width == 2 * FB:
                return FB
            return 512 if self.c % 2 == 0 else 384

        def mine(self, xx):
            return rows(pl.multiple_of(self.c * CHUNK + k * PLANE + xx * SHARE, 16), SHARE)

        def pair_send(self, i):
            theirs = rows(pl.multiple_of(self.c * CHUNK + (1 - k) * PLANE, 16), PLANE)
            cols = rows(i * FB, FB)
            self.pairs[i] = transfer(self.part.at[theirs, cols], self.pair.at[self.c, :, cols], device(dk=1))

        def pair_add(self, i):
            self.pairs[i].wait_recv()
            mine, cols = rows(pl.multiple_of(self.c * CHUNK + k * PLANE, 16), PLANE), rows(i * FB, FB)
            both = self.part[mine, cols].astype(F32) + self.pair[self.c, :, cols].astype(F32)
            self.part[mine, cols] = both.astype(BF16)
            cut, far = self.cut(self.width), self.mine(xo)
            for way, lo, hi, dx in ((0, 0, cut, 1), (1, cut, self.width, -1)):
                if self.width == FB or way == i:
                    self.far[way] = transfer(
                        self.part.at[far, lo:hi], self.r1.at[self.c, :, lo:hi], device(dx=dx)
                    )

        def ring_add(self, i):
            cut = self.cut(self.width)
            xx, lo, hi, dx = ((xp, 0, cut, 1), (xm, cut, self.width, -1))[i]
            self.far[i].wait_recv()
            mine = self.mine(xx)
            both = self.part[mine, lo:hi].astype(F32) + self.r1[self.c, :, lo:hi].astype(F32)
            self.part[mine, lo:hi] = both.astype(BF16)
            self.near[i] = transfer(self.part.at[mine, :], self.r2.at[self.c, i], device(dx=dx))

        def total(self):
            self.near[0].wait_recv()
            self.near[1].wait_recv()
            return (
                self.part[self.mine(x), :].astype(F32)
                + self.r2[self.c, 0].astype(F32)
                + self.r2[self.c, 1].astype(F32)
            )

        def out_send(self):
            own = self.out.at[self.mine(x), :]
            self.side = [
                transfer(own, own, device(dx=1), self.out.at[self.mine(xm), :]),
                transfer(own, own, device(dx=-1), self.out.at[self.mine(xp), :]),
            ]

        def out_forward(self, i):
            cut = self.cut(self.out_width)
            xx, lo, hi, dx = ((xm, 0, cut, 1), (xp, cut, self.out_width, -1))[i]
            self.side[i].wait_recv()
            piece = self.out.at[self.mine(xx), lo:hi]
            self.last[i] = transfer(piece, piece, device(dx=dx), self.out.at[self.mine(xo), lo:hi])

        def out_pair(self):
            self.last[0].wait_recv()
            self.last[1].wait_recv()
            mine = self.out.at[rows(pl.multiple_of(self.c * CHUNK + k * PLANE, 16), PLANE), :]
            theirs = self.out.at[rows(pl.multiple_of(self.c * CHUNK + (1 - k) * PLANE, 16), PLANE), :]
            self.done = transfer(mine, mine, device(dk=1), theirs)

        def out_wait(self):
            if self.done is not None:
                self.done.wait_recv()
                self.done = None

    forward = [RowChunk(c, pre, pre_pair, pre_r1, pre_r2, 2 * FB, hid, FB) for c in range(4)]
    backward = [RowChunk(c, ghp, gh_pair, gh_r1, gh_r2, FB, act, 2 * FB) for c in range(4)]

    def hidden(c):
        both = forward[c].total()
        pre_share[c] = both
        gate, up = both[:, :FB], both[:, FB:]
        hid[forward[c].mine(x), :] = (gate * jax.nn.sigmoid(gate) * up).astype(BF16)
        forward[c].out_send()

    def acts(c):
        grad = backward[c].total()
        gate, up = pre_share[c, :, 0:FB], pre_share[c, :, FB : 2 * FB]
        s = jax.nn.sigmoid(gate)
        mine = backward[c].mine(x)
        act[mine, 0:FB] = (grad * up * s * (1.0 + gate * (1.0 - s))).astype(BF16)
        act[mine, FB : 2 * FB] = (grad * gate * s).astype(BF16)
        backward[c].out_send()

    class ColSum:
        def __init__(self, half, which, part, out):
            self.half, self.part, self.out = half, part, out
            self.c1, self.c2, self.c3 = c1.at[which], c2.at[which], c3.at[which]

        def plane(self, p):
            return p * CHUNK + self.half * PLANE

        def send_far(self):
            start = self.plane(0)
            self.far = [
                transfer(self.part.at[rows(start, 96), :], self.c1.at[0], along(self.half, major=1)),
                transfer(self.part.at[rows(start + 96, 96), :], self.c1.at[1], along(self.half, major=-1)),
            ]
            self.near = [None, None]

        def send_near(self, i):
            self.far[i].wait_recv()
            start = self.plane(1 + i)
            mine = rows(start + i * 96, 96)
            self.part[mine, :] = (self.part[mine, :].astype(F32) + self.c1[i].astype(F32)).astype(BF16)
            self.near[i] = transfer(
                self.part.at[rows(start, PLANE), :], self.c2.at[i], along(self.half, major=1 if i == 0 else -1)
            )

        def send_minor(self):
            self.near[0].wait_recv()
            self.near[1].wait_recv()
            own = rows(self.plane(3), PLANE)
            self.part[own, :] = (
                self.part[own, :].astype(F32) + self.c2[0].astype(F32) + self.c2[1].astype(F32)
            ).astype(BF16)
            self.minor = []
            for m in (1, 2, 3):
                self.minor.append(
                    transfer(
                        self.part.at[rows(self.plane(3) + m * HALF, HALF), :],
                        self.c3.at[m - 1],
                        along(self.half, minor=MINOR_OFF[m]),
                    )
                )

        def store(self):
            total = self.part[rows(self.plane(3), HALF), :].astype(F32)
            for i in range(3):
                self.minor[i].wait_recv()
                total = total + self.c3[i].astype(F32)
            self.out[rows(self.half * HALF, HALF), :] = total.astype(BF16)

    mixed_sum = [ColSum(h, h, part_m, mixed) for h in (0, 1)]
    ginp_sum = [ColSum(h, 2 + h, part_i, ginp) for h in (0, 1)]

    stores = []

    def down_grad(i):
        cols = rows(i * 256, 256)
        gather_g.need(0, 1, 2, 3)
        for c in range(4):
            forward[c].out_wait()
        totals_d[i] = lax.dot_general(hid[...], grads[:, cols], NT, preferred_element_type=F32)
        stores.append(fetch(totals_d.at[i], gdown.at[:, cols]))

    def up_grad(i, first, count):
        cols, part = rows(i % 4 * 256, 256), rows(first * CHUNK, count * CHUNK)
        wide = rows(i // 4 * FB, FB)
        for c in range(first, first + count):
            backward[c].out_wait()
        new = lax.dot_general(xs[part, cols], act[part, wide], NT, preferred_element_type=F32)
        totals_u[cols, wide] = totals_u[cols, wide] + new if first else new

    def up_grad_most(i):
        up_grad(i, 0, 3)

    def up_grad_rest(i):
        up_grad(i, 3, 1)
        cols = rows(i % 4 * 256, 256)
        stores.append(fetch(totals_u.at[cols, rows(i // 4 * FB, FB)], (ggate, gup)[i // 4].at[cols, :]))

    gather_x.begin()
    send_tiles()
    gather_x.forward(0, 0)
    gather_x.spread_on(0, 1)
    gather_x.spread_on(0, 2)
    gather_x.spread_on(1, 1)
    gather_x.spread_on(0, 3)
    gather_x.spread_on(1, 2)
    gather_x.forward(1, 0)
    gather_x.spread_on(1, 3)
    tables()
    gather_g.begin()
    gather_x.forward(1, 1)
    gather_x.forward(0, 1)
    gather_x.forward(0, 2)
    gather_x.forward(1, 2)
    gather_x.forward(0, 3)
    gather_x.forward(1, 3)
    gather_g.spread_on(0, 1)
    permute_most(2)
    permute_most(0)
    gather_g.spread_on(1, 1)
    gather_g.forward(0, 0)
    permute_most(1)
    gather_g.spread_on(1, 2)
    gather_g.spread_on(0, 3)
    gather_g.spread_on(0, 2)
    permute_most(3)
    gather_g.forward(1, 0)
    gather_g.spread_on(1, 3)
    gh_matmul(3)
    permute_rest(0)
    pre_matmul(0, 1)
    backward[3].pair_add(0)
    gather_g.forward(0, 1)
    pre_matmul(0, 0)
    forward[0].pair_add(1)
    gather_g.forward(1, 1)
    permute_rest(1)
    gather_g.forward(1, 2)
    gather_g.forward(0, 3)
    backward[3].ring_add(0)
    backward[3].ring_add(1)
    forward[0].pair_add(0)
    pre_matmul(1, 0)
    gather_g.forward(1, 3)
    gh_matmul(1)
    forward[0].ring_add(1)
    gather_g.forward(0, 2)
    forward[1].pair_add(0)
    pre_matmul(1, 1)
    backward[1].pair_add(0)
    permute_rest(3)
    forward[0].ring_add(0)
    permute_rest(2)
    forward[1].pair_add(1)
    gh_matmul(0)
    pre_matmul(2, 1)
    backward[1].ring_add(0)
    backward[1].ring_add(1)
    backward[0].pair_add(0)
    forward[1].ring_add(0)
    pre_matmul(2, 0)
    forward[2].pair_add(1)
    pre_matmul(3, 0)
    hidden(0)
    forward[2].pair_add(0)
    gh_matmul(2)
    forward[3].pair_add(0)
    backward[0].ring_add(1)
    backward[0].ring_add(0)
    forward[1].ring_add(1)
    pre_matmul(3, 1)
    backward[2].pair_add(0)
    forward[2].ring_add(1)
    forward[0].out_forward(1)
    forward[3].pair_add(1)
    forward[0].out_forward(0)
    forward[2].ring_add(0)
    hidden(1)
    forward[3].ring_add(0)
    acts(1)
    backward[2].ring_add(1)
    acts(0)
    backward[2].ring_add(0)
    forward[0].out_pair()
    mixed_matmul(0)
    mixed_sum[0].send_far()
    mixed_sum[1].send_far()
    hidden(2)
    forward[3].ring_add(1)
    forward[1].out_forward(1)
    forward[1].out_forward(0)
    backward[1].out_forward(1)
    backward[1].out_forward(0)
    backward[0].out_forward(1)
    forward[2].out_forward(1)
    backward[0].out_forward(0)
    acts(2)
    hidden(3)
    forward[2].out_forward(0)
    acts(3)
    forward[1].out_pair()
    mixed_matmul(1)
    mixed_sum[0].send_near(0)
    mixed_sum[1].send_near(0)
    backward[1].out_pair()
    backward[0].out_pair()
    ginp_matmul(1)
    ginp_matmul(0)
    forward[3].out_forward(0)
    ginp_sum[0].send_far()
    backward[2].out_forward(1)
    forward[3].out_forward(1)
    ginp_sum[1].send_far()
    backward[2].out_forward(0)
    forward[2].out_pair()
    mixed_matmul(2)
    mixed_sum[1].send_near(1)
    mixed_sum[0].send_near(1)
    backward[3].out_forward(1)
    backward[3].out_forward(0)
    forward[3].out_pair()
    backward[2].out_pair()
    ginp_sum[0].send_near(0)
    ginp_sum[1].send_near(0)
    down_grad(0)
    ginp_matmul(2)
    ginp_sum[0].send_near(1)
    ginp_sum[1].send_near(1)
    down_grad(1)
    down_grad(3)
    down_grad(2)
    mixed_matmul(3)
    mixed_sum[0].send_minor()
    mixed_sum[1].send_minor()
    backward[3].out_pair()
    up_grad_most(1)
    up_grad_most(5)
    up_grad_most(3)
    up_grad_rest(1)
    up_grad_rest(3)
    ginp_matmul(3)
    up_grad_rest(5)
    ginp_sum[0].send_minor()
    ginp_sum[1].send_minor()
    up_grad_most(6)
    up_grad_rest(6)
    up_grad_most(4)
    up_grad_rest(4)
    up_grad_most(2)
    up_grad_rest(2)
    mixed_sum[0].store()
    mixed_sum[1].store()
    up_grad_most(0)
    up_grad_rest(0)
    up_grad_most(7)
    up_grad_rest(7)
    ginp_sum[1].store()
    ginp_sum[0].store()
    for copy in stores:
        copy.wait()
    for copy in sent:
        if id(copy) not in gone:
            copy.wait_send()


COPIES = 26


def hand_over(*refs):
    sems = refs[10]
    copies = []
    for src, dst in zip(refs[:5], refs[5:10]):
        pieces = 8 if src.dtype == F32 else 1
        size = src.shape[0] // pieces
        for i in range(pieces):
            part = rows(i * size, size)
            copies.append(pltpu.make_async_copy(src.at[part, :], dst.at[part, :], sems.at[len(copies)]))
    for copy in copies:
        copy.start()
    for copy in copies:
        copy.wait()


def per_device(loaded, positions, gate_weight, up_weight, down_weight, segment, log_ratio, token_grad):
    vmem, anywhere = pl.BlockSpec(memory_space=pltpu.VMEM), pl.BlockSpec(memory_space=pl.ANY)
    shape = jax.ShapeDtypeStruct
    buf = lambda *s: pltpu.VMEM(s, BF16)
    transfers = 200
    scratch = [
        pltpu.VMEM((128, 128), F32),
        buf(DB, 2 * FB),
        buf(FB, DB),
        buf(TOK, DB),
        buf(TOK, DB),
        buf(TOK, DB),
        buf(TOK, 2 * FB),
        buf(4, PLANE, 2 * FB),
        buf(4, SHARE, 2 * FB),
        buf(4, 2, SHARE, 2 * FB),
        pltpu.VMEM((4, SHARE, 2 * FB), F32),
        buf(TOK, FB),
        buf(TOK, FB),
        buf(4, PLANE, FB),
        buf(4, SHARE, FB),
        buf(4, 2, SHARE, FB),
        buf(TOK, 2 * FB),
        buf(TOK, DB),
        buf(4, 2, 96, DB),
        buf(4, 2, PLANE, DB),
        buf(4, 3, HALF, DB),
        buf(TOK - FAR, CHUNK),
        buf(FAR, CHUNK),
        pltpu.VMEM((TOK, 128), jnp.int32),
        pltpu.VMEM((DB, 2 * FB), F32),
        pltpu.VMEM((4, FB, 256), F32),
        pltpu.SemaphoreType.DMA((transfers,)),
        pltpu.SemaphoreType.DMA((transfers,)),
        pltpu.SemaphoreType.DMA((16,)),
    ]
    outs = pl.pallas_call(
        kernel,
        out_shape=(
            shape((BLOCK, DB), BF16),
            shape((BLOCK, DB), BF16),
            shape((DB, FB), F32),
            shape((DB, FB), F32),
            shape((FB, DB), F32),
        ),
        in_specs=[vmem] * 5 + [anywhere] * 3,
        out_specs=[vmem] * 2 + [anywhere] * 3,
        scratch_shapes=scratch,
        compiler_params=pltpu.CompilerParams(
            collective_id=0, has_side_effects=True, vmem_limit_bytes=64 * 1024 * 1024
        ),
        name="feed_forward",
    )(
        positions.reshape(1, BLOCK), segment.reshape(1, BLOCK), log_ratio.reshape(1, BLOCK),
        loaded, token_grad, gate_weight, up_weight, down_weight,
    )
    return pl.pallas_call(
        hand_over,
        out_shape=tuple(shape(o.shape, o.dtype) for o in outs),
        in_specs=[anywhere] * 5,
        out_specs=[anywhere] * 5,
        scratch_shapes=[pltpu.SemaphoreType.DMA((COPIES,))],
        name="hand_over",
    )(*outs)


def solution(mesh):
    return jax.shard_map(
        per_device,
        mesh=mesh,
        in_specs=(
            P("col", "row"),
            P("col"),
            P("row", "col"),
            P("row", "col"),
            P("col", "row"),
            P("col"),
            P("col"),
            P("col", "row"),
        ),
        out_specs=(
            P("col", "row"),
            P("col", "row"),
            P("row", "col"),
            P("row", "col"),
            P("col", "row"),
        ),
        check_vma=False,
    )
```

time: 166 us -> 494 us (2.98); the launches traced: 166 us -> 486 us
  Pallas kernels: 150 us -> 485 us
  local copies, waits for them, and re-layouts: 12.7 us -> 0 us
    pallas_call x0 -> x1, Pallas kernels: none -> 347 us  [per_device(): pl.pallas_call(hand_over, out_shape=tuple((shape(o.shape, o.dtype) for o...]
    unnamed x9 -> x0, local copies, waits for them, and re-layouts: 12.7 us -> none
    pallas_call x1, Pallas kernels: 150 us -> 138 us  [per_device(): pl.pallas_call(kernel, out_shape=(shape((BLOCK, DB), BF16), shape((BLOCK,...]
where the time goes in v2:
time: 494 us; the launch traced here: 486 us
  Pallas kernels  485 us (98%)
    pallas_call x1, Pallas kernels, per_device(): pl.pallas_call(hand_over, out_shape=tuple((shape(o.shape, o.dtype) for o...  347 us
    pallas_call x1, Pallas kernels, per_device(): pl.pallas_call(kernel, out_shape=(shape((BLOCK, DB), BF16), shape((BLOCK,...  138 us

profile of v2, /device:TPU:0, one launch (start us, length us, event | category | flops | bytes accessed | tf_op | source)
XLA Modules:
  0.0 485.7 jit_solution(12027877443154477603)
XLA Ops:
  0.6 137.9 %feed_forward.1 = (bf16[96,1024]{1,0:T(8,128)(2,1)}, bf16[96,1024]{1,0:T(8,128)(2,1)}, f32[1024,896]{1,0:T(8,128)}, f32[1024,896]{1,0:T(8,128)}, f32[896,1024]{1,0:T(8,128)}) custom-call(s32[1,96]{1,0:T(1,128)} %bitcast.3, s32[1,96]{1,0:T(1,128)} %bitcast.4, f32[1,96]{1,0:T(1,128)} %bitcast.5, bf16[96,1024]{1,0:T(8,128)(2,1)} %loaded.1, ...), custom_call_target="tpu_custom_call" | custom-call | tf_op jit(solution)/shard_map/feed_forward/pallas_call | solution.py:639
  138.6 346.8 %hand_over.1 = (bf16[96,1024]{1,0:T(8,128)(2,1)}, bf16[96,1024]{1,0:T(8,128)(2,1)}, f32[1024,896]{1,0:T(8,128)}, f32[1024,896]{1,0:T(8,128)}, f32[896,1024]{1,0:T(8,128)}) custom-call(bf16[96,1024]{1,0:T(8,128)(2,1)} %get-tuple-element.10.refs_0_, bf16[96,1024]{1,0:T(8,128)(2,1)} %get-tuple-element.11.refs_1_, f32[1024,896]{1,0:T(8,128)} %get-tuple-element.12.refs_2_, ...), custom_call_target="tpu_custom_call" | custom-call | tf_op jit(solution)/shard_map/hand_over/pallas_call | solution.py:659
